TPU v7x, 32 devices: a whole 2x2x4 slice. The times are simulated.
32 devices in a mesh: seq: 8 (over z, x), chan: 2 (over core), batch: 2 (over y).
Axes of the slice: x: 2, y: 2, z: 4, core: 2. Of those that a mesh axis runs over, the one named last changes fastest.
Arguments:
- gated_input: bfloat16 [2, 1024, 4096], P('batch', 'seq', 'chan'), may hold values from -6 to 6
- query_gate: bfloat16 [2, 1024, 4096], P('batch', 'seq', 'chan'), may hold values from -1.8 to 3.8
- skip_gain: float32 [4096], P('chan'), may hold values from 0.5 to 1.5
- residues: float32 [256, 16], P('chan'), may hold values from -0.25 to 0.25
- decay_rates: float32 [256, 16], P('chan'), may hold values from 9.765625e-07 to 0.12, as said below
- cotangent: bfloat16 [2, 1024, 4096], P('batch', 'seq', 'chan'), may hold values from -200 to 200
Outputs:
- output: bfloat16 [2, 1024, 4096], P('batch', 'seq', 'chan')
- filter_update: float32 [256, 16], P('chan')
Inputs may be any that keep to these rules, and one draw needn't show every extreme that they name: `decay_rates`: decay rate of each filter mode.
All inputs are finite; a program needn't handle non-finite values.
Results may differ from a plain program's by a relative error of at most 0.0052.
Values sent between devices are 32-bit elements; how exact they have to be, the bound alone decides.
A program may use at most 128 MiB of HBM per device.

v0:
```python
import math

import jax
import jax.numpy as jnp
from jax import lax
from jax.sharding import PartitionSpec as P


def carried_in(part, axis, combine, identity):
    place = lax.axis_index(axis)
    gathered = jax.tree.map(lambda a: lax.all_gather(a, axis), part)
    state = jax.tree.map(lambda a, e: jnp.zeros_like(a) + jnp.asarray(e, a.dtype), part, identity)

    def one(turn, state):
        return combine(
            state, jax.tree.map(lambda a: lax.dynamic_index_in_dim(a, turn, 0, False), gathered)
        )

    return lax.fori_loop(0, place, one, state)


def on_device(gated_input, query_gate, skip_gain, residues, decay_rates, cotangent):
    highest = lax.Precision.HIGHEST
    local_batch, steps, chans = gated_input.shape
    groups, modes = residues.shape
    group_width = chans // groups
    group_block = math.gcd(16, groups)
    block_count = groups // group_block
    lag_index = jnp.arange(steps).astype(jnp.float32)
    centred = lag_index - jnp.float32(steps // 2)
    powers = jnp.exp(-decay_rates[:, :, None] * lag_index)
    near_filter = jnp.einsum("gn,gnt->gt", residues, powers, precision=highest).astype(jnp.bfloat16)
    inputs = gated_input.reshape(local_batch, steps, groups, group_width)
    gates = query_gate.astype(jnp.float32).reshape(local_batch, steps, groups, group_width)
    conv_grad = (cotangent.astype(jnp.float32) * query_gate.astype(jnp.float32)).astype(
        jnp.bfloat16
    )
    conv_grad = conv_grad.reshape(local_batch, steps, groups, group_width)
    row_place = jnp.arange(steps)[:, None]
    col_place = jnp.arange(steps)[None, :]
    lower_part = row_place >= col_place
    lag_gap = jnp.maximum(row_place - col_place, 0)

    def block_work(pieces):
        filter_rows, input_rows, grad_rows, rate_rows = pieces
        toeplitz = jnp.where(lower_part[None], filter_rows[:, lag_gap], jnp.zeros((), jnp.bfloat16))
        near_rows = jnp.einsum(
            "gts,bsgw->btgw", toeplitz, input_rows, preferred_element_type=jnp.float32
        )
        pair_sums = jnp.einsum(
            "btgw,bsgw->gts", grad_rows, input_rows, preferred_element_type=jnp.float32
        )
        masked = jnp.where(lower_part[None], pair_sums, jnp.zeros((), jnp.float32))
        rising = jnp.exp(rate_rows[:, :, None] * centred)
        falling = jnp.exp(-rate_rows[:, :, None] * centred)
        partial_rows = jnp.einsum("gts,gns->gtn", masked, rising, precision=highest)
        near_rows_grad = jnp.einsum("gtn,gnt->gn", partial_rows, falling, precision=highest)
        return (near_rows, near_rows_grad)

    split_inputs = jnp.moveaxis(
        inputs.reshape(local_batch, steps, block_count, group_block, group_width), 2, 0
    )
    split_grads = jnp.moveaxis(
        conv_grad.reshape(local_batch, steps, block_count, group_block, group_width), 2, 0
    )
    near_blocks, near_grads = lax.map(
        block_work,
        (
            near_filter.reshape(block_count, group_block, steps),
            split_inputs,
            split_grads,
            decay_rates.reshape(block_count, group_block, modes),
        ),
    )
    near_part = jnp.moveaxis(near_blocks, 0, 2).reshape(local_batch, steps, groups, group_width)
    near_grad = near_grads.reshape(groups, modes)
    end_weight = powers[:, :, ::-1].astype(jnp.bfloat16)
    block_state = jnp.einsum(
        "gnt,btgw->bngw", end_weight, inputs, preferred_element_type=jnp.float32
    ).reshape(local_batch, modes, chans)
    block_decay = jnp.exp(-decay_rates * steps).T

    def combine_carry(earlier, later):
        return (
            earlier[0] * later[0],
            earlier[1] * jnp.repeat(later[0], group_width, axis=1) + later[1],
        )

    identity = (jnp.ones_like(block_decay), jnp.zeros_like(block_state))
    carried = carried_in((block_decay, block_state), "seq", combine_carry, identity)[1]
    carried = carried.reshape(local_batch, modes, groups, group_width)
    start_decay = jnp.exp(-decay_rates[:, :, None] * (lag_index + 1.0))
    start_weight = residues[:, :, None] * start_decay
    far_part = jnp.einsum("gnt,bngw->btgw", start_weight, carried, precision=highest)
    skip_wide = skip_gain.reshape(groups, group_width)
    mixed = gates * (near_part + far_part + skip_wide * inputs.astype(jnp.float32))
    output = mixed.astype(jnp.bfloat16).reshape(local_batch, steps, chans)
    weighted = jnp.einsum(
        "btgw,gnt->bgnw",
        conv_grad,
        start_decay.astype(jnp.bfloat16),
        preferred_element_type=jnp.float32,
    )
    far_grad = jnp.einsum("bgnw,bngw->gn", weighted, carried, precision=highest)
    filter_grad = lax.psum(near_grad + far_grad, ("seq", "batch"))
    square_sum = lax.psum(jnp.sum(filter_grad * filter_grad), "chan")
    grad_length = jnp.sqrt(square_sum + 1e-06)
    clip_limit = jnp.sqrt(jnp.float32(groups * modes * lax.axis_size("chan")))
    return (output, filter_grad * jnp.minimum(1.0, clip_limit / grad_length))


def solution(mesh):
    return jax.shard_map(
        on_device,
        mesh=mesh,
        in_specs=(
            P("batch", "seq", "chan"),
            P("batch", "seq", "chan"),
            P("chan"),
            P("chan", None),
            P("chan", None),
            P("batch", "seq", "chan"),
        ),
        out_specs=(P("batch", "seq", "chan"), P("chan", None)),
        check_vma=False,
    )
```

profile of v0, /device:TPU:0, one launch (start us, length us, event | category | flops | bytes accessed | tf_op | source)
XLA Modules:
  0.0 640.8 jit_solution(10580111036580782832)
XLA Ops:
  7.2 1.3 copy.37
  8.6 0.7 exponential_bitcast_fusion
  9.7 0.4 rev.3
  10.2 0.4 convolution_bitcast_fusion.3
  10.9 1.3 all_gather_reshape.3
  12.5 1.2 fusion.43
  14.4 516.7 %while.27 = (s32[]{:T(128)}, f32[8,1,128,16,16]{2,4,3,1,0:T(8,128)}, f32[8,16,16]{2,1,0:T(8,128)S(1)}, bf16[8,1,128,16,16]{2,4,3,1,0:T(8,128)(2,1)S(1)}, bf16[8,...) while((s32[]{:T(128)}, ...), condition=%wide.region_1.2_spmd.clone.clone, body=%wide.region_0.1_spmd.clone.clone.sunk | while | flops 67879168 | bytes 5268585 | solution.py:66
  14.6 57.4 %gather_fusion = bf16[16384,16]{1,0:T(8,128)(2,1)} fusion(bf16[16,128]{0,1:T(8,128)(2,1)S(1)} %bitcast.123, s32[16384]{0:T(1024)S(1)} %fusion.66), kind=kCustom, calls=%fused_computation.clone.clone.1 | custom fusion | bytes 1114112 | tf_op jit(solution)/shard_map/while/body/eval_jaxpr/gather | solution.py:46
  72.0 3.7 copy.70
  75.7 1.0 fusion.67
  77.2 1.9 fusion.69
  79.2 57.4 %gather_fusion = bf16[16384,16]{1,0:T(8,128)(2,1)} fusion(bf16[16,128]{0,1:T(8,128)(2,1)S(1)} %bitcast.123, s32[16384]{0:T(1024)S(1)} %fusion.66), kind=kCustom, calls=%fused_computation.clone.clone.1 | custom fusion | bytes 1114112 | tf_op jit(solution)/shard_map/while/body/eval_jaxpr/gather | solution.py:46
  136.6 3.7 copy.70
  140.3 1.0 fusion.67
  141.7 1.9 fusion.69
  143.8 57.4 %gather_fusion = bf16[16384,16]{1,0:T(8,128)(2,1)} fusion(bf16[16,128]{0,1:T(8,128)(2,1)S(1)} %bitcast.123, s32[16384]{0:T(1024)S(1)} %fusion.66), kind=kCustom, calls=%fused_computation.clone.clone.1 | custom fusion | bytes 1114112 | tf_op jit(solution)/shard_map/while/body/eval_jaxpr/gather | solution.py:46
  201.2 3.7 copy.70
  204.9 1.1 fusion.67
  206.3 1.9 fusion.69
  208.4 57.4 %gather_fusion = bf16[16384,16]{1,0:T(8,128)(2,1)} fusion(bf16[16,128]{0,1:T(8,128)(2,1)S(1)} %bitcast.123, s32[16384]{0:T(1024)S(1)} %fusion.66), kind=kCustom, calls=%fused_computation.clone.clone.1 | custom fusion | bytes 1114112 | tf_op jit(solution)/shard_map/while/body/eval_jaxpr/gather | solution.py:46
  265.8 3.7 copy.70
  269.5 1.0 fusion.67
  270.9 1.9 fusion.69
  273.0 57.4 %gather_fusion = bf16[16384,16]{1,0:T(8,128)(2,1)} fusion(bf16[16,128]{0,1:T(8,128)(2,1)S(1)} %bitcast.123, s32[16384]{0:T(1024)S(1)} %fusion.66), kind=kCustom, calls=%fused_computation.clone.clone.1 | custom fusion | bytes 1114112 | tf_op jit(solution)/shard_map/while/body/eval_jaxpr/gather | solution.py:46
  330.3 3.7 copy.70
  334.1 1.0 fusion.67
  335.5 1.9 fusion.69
  337.6 57.4 %gather_fusion = bf16[16384,16]{1,0:T(8,128)(2,1)} fusion(bf16[16,128]{0,1:T(8,128)(2,1)S(1)} %bitcast.123, s32[16384]{0:T(1024)S(1)} %fusion.66), kind=kCustom, calls=%fused_computation.clone.clone.1 | custom fusion | bytes 1114112 | tf_op jit(solution)/shard_map/while/body/eval_jaxpr/gather | solution.py:46
  394.9 3.7 copy.70
  398.7 1.0 fusion.67
  400.1 1.9 fusion.69
  402.1 57.4 %gather_fusion = bf16[16384,16]{1,0:T(8,128)(2,1)} fusion(bf16[16,128]{0,1:T(8,128)(2,1)S(1)} %bitcast.123, s32[16384]{0:T(1024)S(1)} %fusion.66), kind=kCustom, calls=%fused_computation.clone.clone.1 | custom fusion | bytes 1114112 | tf_op jit(solution)/shard_map/while/body/eval_jaxpr/gather | solution.py:46
  459.5 3.7 copy.70
  463.3 1.0 fusion.67
  464.7 1.9 fusion.69
  466.7 57.4 %gather_fusion = bf16[16384,16]{1,0:T(8,128)(2,1)} fusion(bf16[16,128]{0,1:T(8,128)(2,1)S(1)} %bitcast.123, s32[16384]{0:T(1024)S(1)} %fusion.66), kind=kCustom, calls=%fused_computation.clone.clone.1 | custom fusion | bytes 1114112 | tf_op jit(solution)/shard_map/while/body/eval_jaxpr/gather | solution.py:46
  524.1 3.7 copy.70
  527.9 1.0 fusion.67
  529.3 1.9 fusion.69
  531.6 32.3 %all-gather = f32[128,128]{1,0:T(8,128)S(1)} all-gather(f32[16,128]{1,0:T(8,128)S(1)} %get-tuple-element.199), channel_id=2, replica_groups=mesh['seq'=8,'chan'=2,'batch'=2] {'seq'}, dimensions={0}, use_global_device_ids=true | all-gather | bytes 73728 | tf_op jit(solution)/shard_map/all_gather | solution.py:11
  563.9 1.5 fusion.35
  565.8 1.7 multiply_reduce_fusion
  567.5 56.2 %psum.14 = f32[128,16]{0,1:T(8,128)S(1)} all-reduce(f32[128,16]{0,1:T(8,128)S(1)} %add.59), channel_id=1, replica_groups=mesh['seq'=8,'chan'=2,'batch'=2] {'seq','batch'}, use_global_device_ids=true, to_apply=%region_4.5 | all-reduce | flops 2048 | bytes 16384 | tf_op jit(solution)/shard_map/psum | solution.py:105
  623.7 0.6 multiply_reduce_fusion.1
  624.3 4.3 fusion.31
  628.6 1.0 copy.49
  629.6 3.1 psum.15
  633.4 0.6 broadcast_multiply_fusion
  (100 shorter events, 6.9 us)
Async XLA Ops:
  7.2 5.1 copy-start.3
  7.2 5.2 copy-start.4
  7.2 558.2 %all-gather.3.cloned.1.call-start = ((), (), s32[]{:S(2)}) async-start(), calls=%async_computation | async-start | bytes 1179648 | tf_op jit(solution)/shard_map/all_gather | solution.py:11
  9.4 4.3 copy-start.1
  9.7 4.2 copy-start.2
  14.4 516.7 %copy-start = (bf16[1,128,2048]{2,1,0:T(8,128)(2,1)S(1)}, bf16[1,128,2048]{2,1,0:T(8,128)(2,1)}, u32[]{:S(2)}) copy-start(bf16[1,128,2048]{2,1,0:T(8,128)(2,1)} %param.10) | copy-start | bytes 1572868
  14.4 517.1 %copy-start.5 = (f32[2048]{0:T(1024)S(1)}, f32[2048]{0:T(1024)}, u32[]{:S(2)}) copy-start(f32[2048]{0:T(1024)} %param.12) | copy-start | bytes 24580
Sparse Core Ops, SparseCore 0:
  12.3 42.8 all-gather.2
where the time goes:
time: 642 us; the launch traced here: 641 us
  local copies, waits for them, and re-layouts  496 us (77%)
  blocking collectives  91.5 us (14%)
  matrix products  33.4 us (5%)
  between operations  15 us (2%)
    gather x16, local copies, waits for them, and re-layouts, block_work(): filter_rows[:, lag_gap]  489 us
    psum x1, blocking collectives, on_device(): filter_grad = lax.psum(near_grad + far_grad, ('seq', 'batch'))  56.2 us
    all_gather x1, blocking collectives, carried_in(): gathered = jax.tree.map(lambda a: lax.all_gather(a, axis), part)  32.3 us
    dot_general x8, matrix products, block_work(): partial_rows = jnp.einsum('gts,gns->gtn', masked, rising, precision=highest)  14.8 us
  transfers between devices with their start and end apart: 1, of which 0 were waited for; matrix products, arithmetic and copies ran while one was open for 81% of the time, Pallas kernels for 0%

commit v1 on v0

v1 whole, which is shorter than its diff:
```python
import functools

import jax
import jax.numpy as jnp
from jax import lax
from jax.experimental import pallas as pl
from jax.experimental.pallas import tpu as pltpu
from jax.sharding import PartitionSpec as P

MESH = pl.DeviceIdType.MESH
F32, BF16 = jnp.float32, jnp.bfloat16
HI = lax.Precision.HIGHEST
LANES = 128
CHUNKS = 2
NN = (((1,), (0,)), ((), ()))
NT = (((1,), (1,)), ((), ()))
TN = (((0,), (0,)), ((), ()))


def dot(a, b, dims=NN, precision=None):
    return lax.dot_general(a, b, dims, precision=precision, preferred_element_type=F32)


def iota(shape, dim):
    return lax.broadcasted_iota(jnp.int32, shape, dim)


def split(a):
    high = a.astype(BF16)
    return high, (a - high.astype(F32)).astype(BF16)


def kernel(
    sizes, rounds, width, modes,
    x_ref, q_ref, ct_ref, skip_ref, res_ref, rate_ref,
    out_ref, upd_ref,
    s_ref, from_mate, dec_ref, filt_ref, q_sum, even_part, chain_in, chain_out,
    own_c, mate_c, other_c, near_ref, grad_in, sd_ref, fall_ref, g_ref, r1, tot_ref, later,
    mate_sem, chain_sem, back_sem, r1_send, r1_recv, later_send, later_recv,
):
    n_seq, n_batch, n_chan = sizes
    pairs = n_seq // 2
    steps, chans = x_ref.shape
    tiles = chans // LANES
    half = tiles // 2
    per = LANES // width
    lane_of = iota((1, LANES), 1)
    seq, bat, cha = (lax.axis_index(a) for a in ("seq", "batch", "chan"))
    parity, line = lax.rem(seq, 2), lax.div(seq, 2)

    def dev(s, b=bat, c=cha):
        return {"seq": s, "batch": b, "chan": c}

    mate = dev(seq + 1 - 2 * parity)
    group_row = iota((LANES, LANES), 0) // width
    group_col = iota((LANES, LANES), 1) // width
    same = group_row == group_col
    lower = iota((steps, steps), 0) >= iota((steps, steps), 1)
    index_sum = iota((steps, steps), 0) + iota((steps, steps), 1)
    corner = index_sum <= steps - 1
    reverse = jnp.where(index_sum == steps - 1, 1.0, 0.0).astype(BF16)
    pick = (iota((per, LANES), 0) == iota((per, LANES), 1) // modes)

    first = [(m & 1, (m >> 1) & 1, (m >> 2) & 1) for m in range(1, 8)]

    def flip(v, bit):
        return 1 - v if bit else v

    first = [(flip(parity, dp), flip(bat, db), flip(cha, dc)) for dp, db, dc in first]
    barrier = pltpu.get_barrier_semaphore()

    def greet(d):
        pl.semaphore_signal(barrier, inc=1, device_id=d, device_id_type=MESH)

    for p, b, c in first:
        greet(dev(2 * line + p, b, c))
    count = len(first)
    hops = []
    for stride, radix in rounds:
        digit = lax.rem(lax.div(line, stride), radix)
        peers = []
        for o in range(1, radix):
            there = lax.rem(digit + o, radix)
            peers.append((there, dev(2 * (line + (there - digit) * stride) + parity)))
        hops.append((digit, peers))
        for _, d in peers:
            greet(d)
        count += radix - 1

    @pl.when(line > 0)
    def _():
        greet(dev(seq - 2))

    @pl.when(line < pairs - 1)
    def _():
        greet(dev(seq + 2))

    count = count + jnp.where(line > 0, 1, 0) + jnp.where(line < pairs - 1, 1, 0)

    back = (steps - 1 - iota((steps, LANES), 0)).astype(F32)
    select = (iota((modes, LANES), 1) % modes) == iota((modes, LANES), 0)
    one_hot = jnp.where(same, 1.0, 0.0).astype(F32)

    def state_tile(h, j):
        i = h * half + j
        at = pl.ds(pl.multiple_of(i * LANES, LANES), LANES)
        lanes = pl.ds(pl.multiple_of(j * LANES, LANES), LANES)
        rate = rate_ref[pl.ds(i, 1), :]
        res = res_ref[pl.ds(i, 1), :]
        falling = jnp.exp(-rate * back)
        fall_ref[i] = falling
        full = dot(falling.astype(BF16), x_ref[:, at], TN)
        full = jnp.where(same, full, 0.0).reshape(per, modes, LANES)
        s_ref[h, :, lanes] = jnp.sum(full, axis=0)
        weight = jnp.where(pick, res, 0.0)
        filt_ref[pl.ds(pl.multiple_of(i * per, per), per), :] = dot(weight, falling, NT, HI)
        decay = jnp.exp(-rate * float(steps))
        dec_ref[h, :, lanes] = dot(jnp.where(select, decay, 0.0), one_hot, NN, HI)

    other = 1 - parity

    def other_tile(j, _):
        state_tile(other, j)
        return 0

    def own_tile(j, _):
        state_tile(parity, j)
        return 0

    lax.fori_loop(0, half, other_tile, 0)
    pl.semaphore_wait(barrier, count)
    to_mate = pltpu.make_async_remote_copy(
        s_ref.at[other], from_mate, mate_sem.at[0], mate_sem.at[1], device_id=mate,
        device_id_type=MESH,
    )
    to_mate.start()
    lax.fori_loop(0, half, own_tile, 0)

    part = half * LANES // CHUNKS

    def chain_copy(k):
        return pltpu.make_async_remote_copy(
            chain_out.at[k], chain_in.at[k], chain_sem.at[0, k], chain_sem.at[1, k],
            device_id=dev(jnp.minimum(seq + 2, n_seq - 1 - (1 - parity))), device_id_type=MESH,
        )

    def back_copy(k):
        return pltpu.make_async_remote_copy(
            mate_c.at[k], other_c.at[k], back_sem.at[0, k], back_sem.at[1, k], device_id=mate,
            device_id_type=MESH,
        )

    def chain_step():
        to_mate.wait_recv()
        for k in range(CHUNKS):
            cols = slice(k * part, (k + 1) * part)
            mine, his = s_ref[parity, :, cols], from_mate[:, cols]
            early = jnp.where(parity == 0, mine, his)
            late = jnp.where(parity == 0, his, mine)
            q_sum[:, cols] = dec_ref[parity, :, cols] * early + late
            even_part[:, cols] = early

        for k in range(CHUNKS):
            cols = slice(k * part, (k + 1) * part)
            decay = dec_ref[parity, :, cols]
            early = even_part[:, cols]

            def finish(carry):
                @pl.when(line < pairs - 1)
                def _():
                    chain_out[k] = decay * decay * carry + q_sum[:, cols]
                    chain_copy(k).start()

                after = decay * carry + early
                mate_c[k] = jnp.where(parity == 0, after, carry)
                back_copy(k).start()
                own_c[k] = jnp.where(parity == 0, carry, after)

            @pl.when(line == 0)
            def _():
                finish(jnp.zeros((modes, part), F32))

            @pl.when(line > 0)
            def _():
                chain_copy(k).wait_recv()
                finish(chain_in[k])

    trigger = jnp.minimum(2 + lax.div(line * tiles, pairs), tiles - 1)
    ahead = (iota((steps, LANES), 0) + 1).astype(F32)

    def near_tile(i, _):
        @pl.when(i == trigger)
        def _():
            chain_step()

        at = pl.ds(pl.multiple_of(i * LANES, LANES), LANES)
        x = x_ref[:, at]
        grad = (ct_ref[:, at].astype(F32) * q_ref[:, at].astype(F32)).astype(BF16)
        grad_in[:, at] = grad
        zero = jnp.zeros((), BF16)
        stacked = jnp.concatenate(
            [jnp.where(lane_of // width == g, x, zero) for g in range(per)], axis=0
        )
        filt = filt_ref[pl.ds(pl.multiple_of(i * per, per), per), :]
        filt = filt.astype(BF16).astype(F32)
        blocks = []
        for g in range(per):
            rows = jnp.broadcast_to(filt[g : g + 1, :], (steps, steps))
            rows = pltpu.roll(rows, 1, 1, stride=1, stride_axis=0)
            blocks.append(jnp.where(lower, rows, 0.0).astype(BF16))
        near = dot(jnp.concatenate(blocks, axis=1), stacked)
        near_ref[:, at] = near + skip_ref[:, at] * x.astype(F32)
        turned = dot(reverse, grad).astype(BF16)
        pair_sums = dot(stacked, turned, NT)
        totals = []
        for g in range(per):
            block = jnp.where(corner, pair_sums[g * steps : (g + 1) * steps], 0.0)
            block = pltpu.roll(block, 0, 1, stride=1, stride_axis=0)
            totals.append(jnp.sum(block, axis=0, keepdims=True))
        lag_sums = jnp.concatenate(totals, axis=0)
        rate = rate_ref[pl.ds(i, 1), :]
        start = jnp.exp(-rate * ahead)
        sd_ref[i] = start
        wide = dot(lag_sums, jnp.where(pick, 1.0, 0.0), TN, HI)
        g_ref[pl.ds(i, 1), :] = jnp.sum(wide * fall_ref[i], axis=0, keepdims=True)
        return 0

    lax.fori_loop(0, tiles, near_tile, 0)

    per_chunk = half // CHUNKS

    def far_tile(h, k, j, carried_ref):
        i = h * half + k * per_chunk + j
        at = pl.ds(pl.multiple_of(i * LANES, LANES), LANES)
        lanes = pl.ds(pl.multiple_of(j * LANES, LANES), LANES)
        carried = carried_ref[k, :, lanes]
        carried = jnp.broadcast_to(carried[None], (per, modes, LANES)).reshape(LANES, LANES)
        c_hi, c_lo = split(jnp.where(same, carried, 0.0))
        start = sd_ref[i]
        a_hi, a_lo = split(res_ref[pl.ds(i, 1), :] * start)
        far = dot(
            jnp.concatenate([a_hi, a_hi, a_lo], axis=1),
            jnp.concatenate([c_hi, c_lo, c_hi], axis=0),
        )
        gate = q_ref[:, at].astype(F32)
        out_ref[:, at] = (gate * (near_ref[:, at] + far)).astype(BF16)
        grad = grad_in[:, at]
        mixed = dot(grad, c_hi, NT) + dot(grad, c_lo, NT)
        gain = jnp.sum(mixed * start.astype(BF16).astype(F32), axis=0, keepdims=True)
        g_ref[pl.ds(i, 1), :] += gain

    def far_loop(h, k, carried_ref):
        def body(j, _):
            far_tile(h, k, j, carried_ref)
            return 0

        lax.fori_loop(0, per_chunk, body, 0)

    for k in range(CHUNKS):
        far_loop(parity, k, own_c)
    for k in range(CHUNKS):
        back_copy(k).wait_recv()
        far_loop(other, k, other_c)

    my_slot = cha * 4 + bat * 2 + parity
    r1[my_slot] = g_ref[...]
    sends = []
    for m, (p, b, c) in enumerate(first):
        copy = pltpu.make_async_remote_copy(
            g_ref, r1.at[my_slot], r1_send.at[m], r1_recv.at[my_slot],
            device_id=dev(2 * line + p, b, c), device_id_type=MESH,
        )
        copy.start()
        sends.append(copy)
    for m, (p, b, c) in enumerate(first):
        slot = c * 4 + b * 2 + p
        pltpu.make_async_remote_copy(
            g_ref, r1.at[slot], r1_send.at[m], r1_recv.at[slot],
            device_id=dev(2 * line + p, b, c), device_id_type=MESH,
        ).wait_recv()
    tot_ref[0, 0] = (r1[0] + r1[1]) + (r1[2] + r1[3])
    tot_ref[0, 1] = (r1[4] + r1[5]) + (r1[6] + r1[7])
    base = 0
    for r, ((stride, radix), (digit, peers)) in enumerate(zip(rounds, hops)):
        here = base + digit
        later[here] = tot_ref[r]
        for o, (there, d) in enumerate(peers):
            copy = pltpu.make_async_remote_copy(
                tot_ref.at[r], later.at[here], later_send.at[base + o], later_recv.at[here],
                device_id=d, device_id_type=MESH,
            )
            copy.start()
            sends.append(copy)
        for o, (there, d) in enumerate(peers):
            pltpu.make_async_remote_copy(
                tot_ref.at[r], later.at[base + there], later_send.at[base + o],
                later_recv.at[base + there], device_id=d, device_id_type=MESH,
            ).wait_recv()
        total = later[base]
        for o in range(1, radix):
            total = total + later[base + o]
        tot_ref[r + 1] = total
        base += radix
    done = len(rounds)
    square = jnp.sum(tot_ref[done] * tot_ref[done], keepdims=True).reshape(1, 1)
    limit = jnp.sqrt(jnp.float32(tiles * LANES * n_chan))
    scale = jnp.minimum(1.0, limit / jnp.sqrt(square + 1e-06))
    upd_ref[...] = tot_ref[done, cha] * scale

    for copy in sends:
        copy.wait_send()
    to_mate.wait_send()
    for k in range(CHUNKS):
        back_copy(k).wait_send()

        @pl.when(line < pairs - 1)
        def _():
            chain_copy(k).wait_send()


def on_device(sizes, gated_input, query_gate, skip_gain, residues, decay_rates, cotangent):
    _, steps, chans = gated_input.shape
    groups, modes = residues.shape
    width = chans // groups
    tiles = chans // LANES
    half = tiles // 2
    pairs = sizes[0] // 2
    rounds, stride = [], 1
    while stride < pairs:
        radix = 4 if (pairs // stride) % 4 == 0 else 2
        rounds.append((stride, radix))
        stride *= radix
    slots = max(1, sum(r for _, r in rounds))
    part = half * LANES // CHUNKS
    wide = half * LANES
    vmem = pl.BlockSpec(memory_space=pltpu.VMEM)
    dma = pltpu.SemaphoreType.DMA
    output, update = pl.pallas_call(
        functools.partial(kernel, sizes, rounds, width, modes),
        out_shape=(
            jax.ShapeDtypeStruct((steps, chans), BF16),
            jax.ShapeDtypeStruct((tiles, LANES), F32),
        ),
        in_specs=[vmem] * 6,
        out_specs=(vmem, vmem),
        scratch_shapes=[
            pltpu.VMEM((2, modes, wide), F32),
            pltpu.VMEM((modes, wide), F32),
            pltpu.VMEM((2, modes, wide), F32),
            pltpu.VMEM((groups, steps), F32),
            pltpu.VMEM((modes, wide), F32),
            pltpu.VMEM((modes, wide), F32),
            pltpu.VMEM((CHUNKS, modes, part), F32),
            pltpu.VMEM((CHUNKS, modes, part), F32),
            pltpu.VMEM((CHUNKS, modes, part), F32),
            pltpu.VMEM((CHUNKS, modes, part), F32),
            pltpu.VMEM((CHUNKS, modes, part), F32),
            pltpu.VMEM((steps, chans), F32),
            pltpu.VMEM((steps, chans), BF16),
            pltpu.VMEM((tiles, steps, LANES), F32),
            pltpu.VMEM((tiles, steps, LANES), F32),
            pltpu.VMEM((tiles, LANES), F32),
            pltpu.VMEM((8, tiles, LANES), F32),
            pltpu.VMEM((len(rounds) + 1, 2, tiles, LANES), F32),
            pltpu.VMEM((slots, 2, tiles, LANES), F32),
            dma((2,)),
            dma((2, CHUNKS)),
            dma((2, CHUNKS)),
            dma((7,)),
            dma((8,)),
            dma((slots,)),
            dma((slots,)),
        ],
        compiler_params=pltpu.CompilerParams(
            collective_id=0, has_side_effects=True, vmem_limit_bytes=48 * 1024 * 1024
        ),
    )(
        gated_input.reshape(steps, chans),
        query_gate.reshape(steps, chans),
        cotangent.reshape(steps, chans),
        skip_gain.reshape(1, chans),
        residues.reshape(tiles, LANES),
        decay_rates.reshape(tiles, LANES),
    )
    return output.reshape(gated_input.shape), update.reshape(groups, modes)


def solution(mesh):
    sizes = tuple(mesh.shape[a] for a in ("seq", "batch", "chan"))
    return jax.shard_map(
        functools.partial(on_device, sizes),
        mesh=mesh,
        in_specs=(
            P("batch", "seq", "chan"),
            P("batch", "seq", "chan"),
            P("chan"),
            P("chan", None),
            P("chan", None),
            P("batch", "seq", "chan"),
        ),
        out_specs=(P("batch", "seq", "chan"), P("chan", None)),
        check_vma=False,
    )
```

time: 642 us -> 43.6 us (0.07)
  local copies, waits for them, and re-layouts: 496 us -> 6.94 us
  blocking collectives: 91.5 us -> 0 us
  Pallas kernels: 0 us -> 35.6 us
  matrix products: 33.4 us -> 0 us
  between operations: 15 us -> 0.66 us
    gather x16 -> x0, local copies, waits for them, and re-layouts: 489 us -> none  [block_work(): filter_rows[:, lag_gap]]
    psum x2 -> x0, blocking collectives: 59.2 us -> none  [the longest x1 56.2 us: on_device(): filter_grad = lax.psum(near_grad + far_grad, ('seq', 'batch'))]
    pallas_call x0 -> x1, Pallas kernels: none -> 35.6 us  [on_device(): pl.pallas_call(functools.partial(kernel, sizes, rounds, width, modes), ou...]
    dot_general x28 -> x0, matrix products: 33.4 us -> none  [the longest x8 14.8 us: block_work(): partial_rows = jnp.einsum('gts,gns->gtn', masked, rising, precision=highest)]
    all_gather x1 -> x0, blocking collectives: 32.3 us -> none  [carried_in(): gathered = jax.tree.map(lambda a: lax.all_gather(a, axis), part)]
  transfers between devices with their start and end apart: 1 -> 0, of which waited for: 0 -> 0; matrix products, arithmetic and copies ran while one was open for 81% -> 0% of each run, Pallas kernels for 0% -> 0%
where the time goes in v1:
time: 43.6 us; the launch traced here: 43.2 us
  Pallas kernels  35.6 us (82%)
  local copies, waits for them, and re-layouts  6.94 us (16%)
  between operations  0.66 us (2%)
    pallas_call x1, Pallas kernels, on_device(): pl.pallas_call(functools.partial(kernel, sizes, rounds, width, modes), ou...  35.6 us
    unnamed x14, local copies, waits for them, and re-layouts  6.71 us

profile of v1, /device:TPU:0, one launch (start us, length us, event | category | flops | bytes accessed | tf_op | source)
XLA Modules:
  0.0 43.2 jit_solution(377583835120541247)
XLA Ops:
  0.6 0.8 %copy.11 = f32[128,16]{1,0:T(8,128)S(1)} copy(f32[128,16]{0,1:T(8,128)} %param.9) | data formatting | bytes 16384 | tf_op args[3]
  1.4 0.0 copy-start.4
  1.4 0.1 reshape.32.res_ref
  1.5 0.6 %copy-done.4 = f32[128,16]{0,1:T(8,128)S(1)} copy-done((f32[128,16]{0,1:T(8,128)S(1)}, f32[128,16]{0,1:T(8,128)}, u32[]{:S(2)}) %copy-start.4) | copy-done | bytes 8216
  2.1 0.1 copy.12
  2.2 0.0 copy-start.3
  2.2 0.1 reshape.33.rate_ref
  2.3 0.6 %copy-done.3 = f32[2048]{0:T(1024)S(1)} copy-done((f32[2048]{0:T(1024)S(1)}, f32[2048]{0:T(1024)}, u32[]{:S(2)}) %copy-start.3) | copy-done | bytes 8216
  2.9 0.0 copy-start
  2.9 1.0 %copy-done = bf16[1,128,2048]{2,1,0:T(8,128)(2,1)S(1)} copy-done((bf16[1,128,2048]{2,1,0:T(8,128)(2,1)S(1)}, bf16[1,128,2048]{2,1,0:T(8,128)(2,1)}, u32[]{:S(2)}) %copy-start) | copy-done | bytes 524312
  4.0 0.0 copy-start.1
  4.0 1.0 %copy-done.1 = bf16[1,128,2048]{2,1,0:T(8,128)(2,1)S(1)} copy-done((bf16[1,128,2048]{2,1,0:T(8,128)(2,1)S(1)}, bf16[1,128,2048]{2,1,0:T(8,128)(2,1)}, u32[]{:S(2)}) %copy-start.1) | copy-done | bytes 524312
  5.0 0.0 copy-start.2
  5.0 1.0 %copy-done.2 = bf16[1,128,2048]{2,1,0:T(8,128)(2,1)S(1)} copy-done((bf16[1,128,2048]{2,1,0:T(8,128)(2,1)S(1)}, bf16[1,128,2048]{2,1,0:T(8,128)(2,1)}, u32[]{:S(2)}) %copy-start.2) | copy-done | bytes 524312
  6.0 35.6 %shard_map.77 = (bf16[128,2048]{1,0:T(8,128)(2,1)S(1)}, f32[16,128]{1,0:T(8,128)S(1)}) custom-call(bf16[128,2048]{1,0:T(8,128)(2,1)S(1)} %bitcast.5, bf16[128,2048]{1,0:T(8,128)(2,1)S(1)} %bitcast.6, bf16[128,2048]{1,0:T(8,128)(2,1)S(1)} %bitcast.7, f32[1,2048]{1,0:T(1,128)S(1)} %bitcast.9, f32[16,128]{1,0:T(8,128)S(1)} %reshape.32.res_ref, ...), custom_call_target="tpu_custom_call" | custom-call | tf_op jit(solution)/shard_map/pallas_call | solution.py:338
  41.7 0.1 reshape.35
  41.7 0.7 %copy.13 = f32[128,16]{0,1:T(8,128)} copy(f32[128,16]{1,0:T(8,128)S(1)} %reshape.35) | data formatting | bytes 16384
  42.4 0.8 %copy.15 = bf16[1,128,2048]{2,1,0:T(8,128)(2,1)} copy(bf16[1,128,2048]{2,1,0:T(8,128)(2,1)S(1)} %bitcast.8) | data formatting | bytes 1048576
Async XLA Ops:
  1.4 0.7 %copy-start.4 = (f32[128,16]{0,1:T(8,128)S(1)}, f32[128,16]{0,1:T(8,128)}, u32[]{:S(2)}) copy-start(f32[128,16]{0,1:T(8,128)} %param.10) | copy-start | bytes 24580
  2.2 0.7 %copy-start.3 = (f32[2048]{0:T(1024)S(1)}, f32[2048]{0:T(1024)}, u32[]{:S(2)}) copy-start(f32[2048]{0:T(1024)} %param.8) | copy-start | bytes 24580
  2.9 1.0 %copy-start = (bf16[1,128,2048]{2,1,0:T(8,128)(2,1)S(1)}, bf16[1,128,2048]{2,1,0:T(8,128)(2,1)}, u32[]{:S(2)}) copy-start(bf16[1,128,2048]{2,1,0:T(8,128)(2,1)} %param.6) | copy-start | bytes 1572868
  4.0 1.0 %copy-start.1 = (bf16[1,128,2048]{2,1,0:T(8,128)(2,1)S(1)}, bf16[1,128,2048]{2,1,0:T(8,128)(2,1)}, u32[]{:S(2)}) copy-start(bf16[1,128,2048]{2,1,0:T(8,128)(2,1)} %param.7) | copy-start | bytes 1572868
  5.0 1.0 %copy-start.2 = (bf16[1,128,2048]{2,1,0:T(8,128)(2,1)S(1)}, bf16[1,128,2048]{2,1,0:T(8,128)(2,1)}, u32[]{:S(2)}) copy-start(bf16[1,128,2048]{2,1,0:T(8,128)(2,1)} %param.11) | copy-start | bytes 1572868

commit v2 on v1

--- a/solution.py
+++ b/solution.py
@@ -30,17 +30,30 @@
     return high, (a - high.astype(F32)).astype(BF16)
 
 
+def split3(a):
+    high, rest = a.astype(BF16), a
+    rest = a - high.astype(F32)
+    mid = rest.astype(BF16)
+    return high, mid, (rest - mid.astype(F32)).astype(BF16)
+
+
+def rows_by_one_hot(parts, one_hot):
+    stacked = jnp.concatenate([p.astype(F32) for p in parts], axis=0).astype(BF16)
+    return stacked, jnp.concatenate([one_hot] * len(parts), axis=0)
+
+
 def kernel(
     sizes, rounds, width, modes,
-    x_ref, q_ref, ct_ref, skip_ref, res_ref, rate_ref,
+    x_hbm, q_hbm, ct_hbm, skip_hbm, res_hbm, rate_hbm,
     out_ref, upd_ref,
+    x_ref, q_ref, ct_ref, skip_ref, res_in, rate_in, res_ref, rate_ref, in_sem,
     s_ref, from_mate, dec_ref, filt_ref, q_sum, even_part, chain_in, chain_out,
     own_c, mate_c, other_c, near_ref, grad_in, sd_ref, fall_ref, g_ref, r1, tot_ref, later,
     mate_sem, chain_sem, back_sem, r1_send, r1_recv, later_send, later_recv,
 ):
     n_seq, n_batch, n_chan = sizes
     pairs = n_seq // 2
-    steps, chans = x_ref.shape
+    steps, chans = x_hbm.shape
     tiles = chans // LANES
     half = tiles // 2
     per = LANES // width
@@ -50,6 +63,23 @@
 
     def dev(s, b=bat, c=cha):
         return {"seq": s, "batch": b, "chan": c}
+
+    def fetch(n, src, dst):
+        copy = pltpu.make_async_copy(src, dst, in_sem.at[n])
+        copy.start()
+        return copy
+
+    def columns(h):
+        return pl.ds(pl.multiple_of(h * (half * LANES), LANES), half * LANES)
+
+    other = 1 - parity
+    get_rate = fetch(0, rate_hbm, rate_in)
+    get_res = fetch(1, res_hbm, res_in)
+    get_x1 = fetch(2, x_hbm.at[:, columns(other)], x_ref.at[:, columns(other)])
+    get_x2 = fetch(3, x_hbm.at[:, columns(parity)], x_ref.at[:, columns(parity)])
+    get_q = fetch(4, q_hbm, q_ref)
+    get_ct = fetch(5, ct_hbm, ct_ref)
+    get_skip = fetch(6, skip_hbm, skip_ref)
 
     mate = dev(seq + 1 - 2 * parity)
     group_row = iota((LANES, LANES), 0) // width
@@ -99,7 +129,7 @@
 
     back = (steps - 1 - iota((steps, LANES), 0)).astype(F32)
     select = (iota((modes, LANES), 1) % modes) == iota((modes, LANES), 0)
-    one_hot = jnp.where(same, 1.0, 0.0).astype(F32)
+    one_hot = jnp.where(same, 1.0, 0.0).astype(BF16)
 
     def state_tile(h, j):
         i = h * half + j
@@ -109,32 +139,58 @@
         res = res_ref[pl.ds(i, 1), :]
         falling = jnp.exp(-rate * back)
         fall_ref[i] = falling
-        full = dot(falling.astype(BF16), x_ref[:, at], TN)
+        f_hi, f_lo = split(falling)
+        full = dot(f_hi, x_ref[:, at], TN)
         full = jnp.where(same, full, 0.0).reshape(per, modes, LANES)
         s_ref[h, :, lanes] = jnp.sum(full, axis=0)
-        weight = jnp.where(pick, res, 0.0)
-        filt_ref[pl.ds(pl.multiple_of(i * per, per), per), :] = dot(weight, falling, NT, HI)
+        w_hi, w_lo = split(jnp.where(pick, res, 0.0))
+        filt_ref[pl.ds(pl.multiple_of(i * per, per), per), :] = dot(
+            jnp.concatenate([w_hi, w_hi, w_lo], axis=1),
+            jnp.concatenate([f_hi, f_lo, f_hi], axis=1),
+            NT,
+        )
         decay = jnp.exp(-rate * float(steps))
-        dec_ref[h, :, lanes] = dot(jnp.where(select, decay, 0.0), one_hot, NN, HI)
-
-    other = 1 - parity
-
-    def other_tile(j, _):
-        state_tile(other, j)
+        spread = dot(
+            jnp.concatenate(split3(jnp.where(select, decay, 0.0)), axis=0), one_hot
+        )
+        dec_ref[h, :, lanes] = spread[:modes] + spread[modes : 2 * modes] + spread[2 * modes :]
+
+    def other_two(j, _):
+        state_tile(other, 2 * j)
+        state_tile(other, 2 * j + 1)
         return 0
 
-    def own_tile(j, _):
-        state_tile(parity, j)
+    def own_two(j, _):
+        state_tile(parity, 2 * j)
+        state_tile(parity, 2 * j + 1)
         return 0
 
-    lax.fori_loop(0, half, other_tile, 0)
+    groups = tiles * per
+    row_group = lax.rem(iota((groups, LANES), 0), per) == iota((groups, LANES), 1) // modes
+    mode_hot = jnp.where(select, 1.0, 0.0).astype(BF16)
+
+    def by_rows(ref):
+        left, right = rows_by_one_hot(split3(ref[...]), mode_hot)
+        wide = jnp.where(row_group, dot(left, right, TN), 0.0)
+        return jnp.sum(wide.reshape(tiles, per, LANES), axis=1)
+
+    get_rate.wait()
+    rate_ref[...] = by_rows(rate_in)
+    get_res.wait()
+    res_ref[...] = by_rows(res_in)
+    get_x1.wait()
+    lax.fori_loop(0, half // 2, other_two, 0)
     pl.semaphore_wait(barrier, count)
     to_mate = pltpu.make_async_remote_copy(
         s_ref.at[other], from_mate, mate_sem.at[0], mate_sem.at[1], device_id=mate,
         device_id_type=MESH,
     )
     to_mate.start()
-    lax.fori_loop(0, half, own_tile, 0)
+    get_x2.wait()
+    lax.fori_loop(0, half // 2, own_two, 0)
+    get_q.wait()
+    get_ct.wait()
+    get_skip.wait()
 
     part = half * LANES // CHUNKS
 
@@ -185,14 +241,10 @@
                 chain_copy(k).wait_recv()
                 finish(chain_in[k])
 
-    trigger = jnp.minimum(2 + lax.div(line * tiles, pairs), tiles - 1)
+    trigger = jnp.minimum(1 + lax.div(line * half, pairs), half - 1)
     ahead = (iota((steps, LANES), 0) + 1).astype(F32)
 
-    def near_tile(i, _):
-        @pl.when(i == trigger)
-        def _():
-            chain_step()
-
+    def near_tile(i):
         at = pl.ds(pl.multiple_of(i * LANES, LANES), LANES)
         x = x_ref[:, at]
         grad = (ct_ref[:, at].astype(F32) * q_ref[:, at].astype(F32)).astype(BF16)
@@ -221,11 +273,20 @@
         rate = rate_ref[pl.ds(i, 1), :]
         start = jnp.exp(-rate * ahead)
         sd_ref[i] = start
-        wide = dot(lag_sums, jnp.where(pick, 1.0, 0.0), TN, HI)
+        left, right = rows_by_one_hot(split3(lag_sums), jnp.where(pick, 1.0, 0.0))
+        wide = dot(left, right.astype(BF16), TN)
         g_ref[pl.ds(i, 1), :] = jnp.sum(wide * fall_ref[i], axis=0, keepdims=True)
+
+    def near_two(i, _):
+        @pl.when(i == trigger)
+        def _():
+            chain_step()
+
+        near_tile(2 * i)
+        near_tile(2 * i + 1)
         return 0
 
-    lax.fori_loop(0, tiles, near_tile, 0)
+    lax.fori_loop(0, half, near_two, 0)
 
     per_chunk = half // CHUNKS
 
@@ -251,10 +312,11 @@
 
     def far_loop(h, k, carried_ref):
         def body(j, _):
-            far_tile(h, k, j, carried_ref)
+            far_tile(h, k, 2 * j, carried_ref)
+            far_tile(h, k, 2 * j + 1, carried_ref)
             return 0
 
-        lax.fori_loop(0, per_chunk, body, 0)
+        lax.fori_loop(0, per_chunk // 2, body, 0)
 
     for k in range(CHUNKS):
         far_loop(parity, k, own_c)
@@ -305,7 +367,10 @@
     square = jnp.sum(tot_ref[done] * tot_ref[done], keepdims=True).reshape(1, 1)
     limit = jnp.sqrt(jnp.float32(tiles * LANES * n_chan))
     scale = jnp.minimum(1.0, limit / jnp.sqrt(square + 1e-06))
-    upd_ref[...] = tot_ref[done, cha] * scale
+    rows = tot_ref[done, cha] * scale
+    rows = jnp.broadcast_to(rows[:, None, :], (tiles, per, LANES)).reshape(groups, LANES)
+    rows = jnp.concatenate(split3(jnp.where(row_group, rows, 0.0)), axis=1)
+    upd_ref[...] = dot(jnp.concatenate([mode_hot] * 3, axis=1), rows, NT)
 
     for copy in sends:
         copy.wait_send()
@@ -339,11 +404,20 @@
         functools.partial(kernel, sizes, rounds, width, modes),
         out_shape=(
             jax.ShapeDtypeStruct((steps, chans), BF16),
-            jax.ShapeDtypeStruct((tiles, LANES), F32),
+            jax.ShapeDtypeStruct((modes, groups), F32),
         ),
-        in_specs=[vmem] * 6,
+        in_specs=[pl.BlockSpec(memory_space=pltpu.HBM)] * 6,
         out_specs=(vmem, vmem),
         scratch_shapes=[
+            pltpu.VMEM((steps, chans), BF16),
+            pltpu.VMEM((steps, chans), BF16),
+            pltpu.VMEM((steps, chans), BF16),
+            pltpu.VMEM((1, chans), F32),
+            pltpu.VMEM((modes, groups), F32),
+            pltpu.VMEM((modes, groups), F32),
+            pltpu.VMEM((tiles, LANES), F32),
+            pltpu.VMEM((tiles, LANES), F32),
+            dma((7,)),
             pltpu.VMEM((2, modes, wide), F32),
             pltpu.VMEM((modes, wide), F32),
             pltpu.VMEM((2, modes, wide), F32),
@@ -379,10 +453,10 @@
         query_gate.reshape(steps, chans),
         cotangent.reshape(steps, chans),
         skip_gain.reshape(1, chans),
-        residues.reshape(tiles, LANES),
-        decay_rates.reshape(tiles, LANES),
+        residues.T,
+        decay_rates.T,
     )
-    return output.reshape(gated_input.shape), update.reshape(groups, modes)
+    return output.reshape(gated_input.shape), update.T
 
 
 def solution(mesh):

time: 43.6 us -> 37.4 us (0.86)
  Pallas kernels: 35.6 us -> 29.7 us
    pallas_call x1, Pallas kernels: 35.6 us -> 29.7 us  [on_device(): pl.pallas_call(functools.partial(kernel, sizes, rounds, width, modes), ou...]
where the time goes in v2:
time: 37.4 us; the launch traced here: 37 us
  Pallas kernels  29.7 us (79%)
  local copies, waits for them, and re-layouts  6.6 us (18%)
  between operations  0.65 us (2%)
    pallas_call x1, Pallas kernels, on_device(): pl.pallas_call(functools.partial(kernel, sizes, rounds, width, modes), ou...  29.7 us
    unnamed x14, local copies, waits for them, and re-layouts  6.6 us

profile of v2, /device:TPU:0, one launch (start us, length us, event | category | flops | bytes accessed | tf_op | source)
XLA Modules:
  0.0 37.0 jit_solution(7519042541621478296)
XLA Ops:
  0.6 0.0 copy-start.3
  0.6 0.7 %copy-done.3 = f32[2048]{0:T(1024)S(1)} copy-done((f32[2048]{0:T(1024)S(1)}, f32[2048]{0:T(1024)}, u32[]{:S(2)}) %copy-start.3) | copy-done | bytes 8216
  1.3 0.0 copy-start
  1.3 1.0 %copy-done = bf16[1,128,2048]{2,1,0:T(8,128)(2,1)S(1)} copy-done((bf16[1,128,2048]{2,1,0:T(8,128)(2,1)S(1)}, bf16[1,128,2048]{2,1,0:T(8,128)(2,1)}, u32[]{:S(2)}) %copy-start) | copy-done | bytes 524312
  2.4 0.0 copy-start.1
  2.4 1.0 %copy-done.1 = bf16[1,128,2048]{2,1,0:T(8,128)(2,1)S(1)} copy-done((bf16[1,128,2048]{2,1,0:T(8,128)(2,1)S(1)}, bf16[1,128,2048]{2,1,0:T(8,128)(2,1)}, u32[]{:S(2)}) %copy-start.1) | copy-done | bytes 524312
  3.4 0.0 copy-start.2
  3.4 1.0 %copy-done.2 = bf16[1,128,2048]{2,1,0:T(8,128)(2,1)S(1)} copy-done((bf16[1,128,2048]{2,1,0:T(8,128)(2,1)S(1)}, bf16[1,128,2048]{2,1,0:T(8,128)(2,1)}, u32[]{:S(2)}) %copy-start.2) | copy-done | bytes 524312
  4.5 0.0 copy-start.4
  4.5 0.7 %copy-done.4 = f32[128,16]{0,1:T(8,128)S(1)} copy-done((f32[128,16]{0,1:T(8,128)S(1)}, f32[128,16]{0,1:T(8,128)}, u32[]{:S(2)}) %copy-start.4) | copy-done | bytes 8216
  5.2 0.0 copy-start.5
  5.2 0.7 %copy-done.5 = f32[128,16]{0,1:T(8,128)S(1)} copy-done((f32[128,16]{0,1:T(8,128)S(1)}, f32[128,16]{0,1:T(8,128)}, u32[]{:S(2)}) %copy-start.5) | copy-done | bytes 8216
  5.9 29.7 %shard_map.77 = (bf16[128,2048]{1,0:T(8,128)(2,1)S(1)}, f32[16,128]{1,0:T(8,128)S(1)}) custom-call(bf16[128,2048]{1,0:T(8,128)(2,1)S(1)} %bitcast.8, bf16[128,2048]{1,0:T(8,128)(2,1)S(1)} %bitcast.9, bf16[128,2048]{1,0:T(8,128)(2,1)S(1)} %bitcast.10, f32[1,2048]{1,0:T(1,128)S(1)} %bitcast.12, f32[16,128]{1,0:T(8,128)S(1)} %bitcast.13, f32[16,128]{1,0:T(8,128)S(1)} %bitcast.14), custom_call_target="tpu_custom_call" | custom-call | tf_op jit(solution)/shard_map/pallas_call | solution.py:403
  35.6 0.8 %copy.10 = bf16[1,128,2048]{2,1,0:T(8,128)(2,1)} copy(bf16[1,128,2048]{2,1,0:T(8,128)(2,1)S(1)} %bitcast.11) | data formatting | bytes 1048576
  36.4 0.6 %copy.11 = f32[128,16]{0,1:T(8,128)} copy(f32[128,16]{0,1:T(8,128)S(1)} %bitcast.15) | data formatting | bytes 16384
Async XLA Ops:
  0.6 0.7 %copy-start.3 = (f32[2048]{0:T(1024)S(1)}, f32[2048]{0:T(1024)}, u32[]{:S(2)}) copy-start(f32[2048]{0:T(1024)} %param.8) | copy-start | bytes 24580
  1.3 1.0 %copy-start = (bf16[1,128,2048]{2,1,0:T(8,128)(2,1)S(1)}, bf16[1,128,2048]{2,1,0:T(8,128)(2,1)}, u32[]{:S(2)}) copy-start(bf16[1,128,2048]{2,1,0:T(8,128)(2,1)} %param.6) | copy-start | bytes 1572868
  2.4 1.0 %copy-start.1 = (bf16[1,128,2048]{2,1,0:T(8,128)(2,1)S(1)}, bf16[1,128,2048]{2,1,0:T(8,128)(2,1)}, u32[]{:S(2)}) copy-start(bf16[1,128,2048]{2,1,0:T(8,128)(2,1)} %param.7) | copy-start | bytes 1572868
  3.4 1.0 %copy-start.2 = (bf16[1,128,2048]{2,1,0:T(8,128)(2,1)S(1)}, bf16[1,128,2048]{2,1,0:T(8,128)(2,1)}, u32[]{:S(2)}) copy-start(bf16[1,128,2048]{2,1,0:T(8,128)(2,1)} %param.11) | copy-start | bytes 1572868
  4.5 0.7 %copy-start.4 = (f32[128,16]{0,1:T(8,128)S(1)}, f32[128,16]{0,1:T(8,128)}, u32[]{:S(2)}) copy-start(f32[128,16]{0,1:T(8,128)} %param.9) | copy-start | bytes 24580
  5.2 0.7 %copy-start.5 = (f32[128,16]{0,1:T(8,128)S(1)}, f32[128,16]{0,1:T(8,128)}, u32[]{:S(2)}) copy-start(f32[128,16]{0,1:T(8,128)} %param.10) | copy-start | bytes 24580

commit v3 on v2

--- a/solution.py
+++ b/solution.py
@@ -11,7 +11,7 @@
 F32, BF16 = jnp.float32, jnp.bfloat16
 HI = lax.Precision.HIGHEST
 LANES = 128
-CHUNKS = 2
+CHUNKS = 4
 NN = (((1,), (0,)), ((), ()))
 NT = (((1,), (1,)), ((), ()))
 TN = (((0,), (0,)), ((), ()))
@@ -43,13 +43,13 @@
 
 
 def kernel(
-    sizes, rounds, width, modes,
+    sizes, width, modes,
     x_hbm, q_hbm, ct_hbm, skip_hbm, res_hbm, rate_hbm,
     out_ref, upd_ref,
     x_ref, q_ref, ct_ref, skip_ref, res_in, rate_in, res_ref, rate_ref, in_sem,
     s_ref, from_mate, dec_ref, filt_ref, q_sum, even_part, chain_in, chain_out,
-    own_c, mate_c, other_c, near_ref, grad_in, sd_ref, fall_ref, g_ref, r1, tot_ref, later,
-    mate_sem, chain_sem, back_sem, r1_send, r1_recv, later_send, later_recv,
+    own_c, mate_c, other_c, near_ref, grad_in, sd_ref, fall_ref, g_ref, all_g, tot_ref,
+    mate_sem, chain_sem, back_sem, g_send, g_recv, twin_sem,
 ):
     n_seq, n_batch, n_chan = sizes
     pairs = n_seq // 2
@@ -91,31 +91,26 @@
     reverse = jnp.where(index_sum == steps - 1, 1.0, 0.0).astype(BF16)
     pick = (iota((per, LANES), 0) == iota((per, LANES), 1) // modes)
 
-    first = [(m & 1, (m >> 1) & 1, (m >> 2) & 1) for m in range(1, 8)]
-
-    def flip(v, bit):
-        return 1 - v if bit else v
-
-    first = [(flip(parity, dp), flip(bat, db), flip(cha, dc)) for dp, db, dc in first]
     barrier = pltpu.get_barrier_semaphore()
 
     def greet(d):
         pl.semaphore_signal(barrier, inc=1, device_id=d, device_id_type=MESH)
 
-    for p, b, c in first:
-        greet(dev(2 * line + p, b, c))
-    count = len(first)
-    hops = []
-    for stride, radix in rounds:
-        digit = lax.rem(lax.div(line, stride), radix)
-        peers = []
-        for o in range(1, radix):
-            there = lax.rem(digit + o, radix)
-            peers.append((there, dev(2 * (line + (there - digit) * stride) + parity)))
-        hops.append((digit, peers))
-        for _, d in peers:
-            greet(d)
-        count += radix - 1
+    members = n_seq * n_batch
+    me = bat * n_seq + seq
+    twin = dev(seq, bat, 1 - cha)
+
+    def member(m):
+        there = lax.rem(me + m, members)
+        return there, dev(lax.rem(there, n_seq), lax.div(there, n_seq))
+
+    def greet_member(m, _):
+        greet(member(m)[1])
+        return 0
+
+    lax.fori_loop(1, members, greet_member, 0)
+    greet(twin)
+    count = members
 
     @pl.when(line > 0)
     def _():
@@ -316,7 +311,7 @@
             far_tile(h, k, 2 * j + 1, carried_ref)
             return 0
 
-        lax.fori_loop(0, per_chunk // 2, body, 0)
+        lax.fori_loop(0, max(1, per_chunk // 2), body, 0)
 
     for k in range(CHUNKS):
         far_loop(parity, k, own_c)
@@ -324,56 +319,47 @@
         back_copy(k).wait_recv()
         far_loop(other, k, other_c)
 
-    my_slot = cha * 4 + bat * 2 + parity
-    r1[my_slot] = g_ref[...]
-    sends = []
-    for m, (p, b, c) in enumerate(first):
-        copy = pltpu.make_async_remote_copy(
-            g_ref, r1.at[my_slot], r1_send.at[m], r1_recv.at[my_slot],
-            device_id=dev(2 * line + p, b, c), device_id_type=MESH,
-        )
-        copy.start()
-        sends.append(copy)
-    for m, (p, b, c) in enumerate(first):
-        slot = c * 4 + b * 2 + p
-        pltpu.make_async_remote_copy(
-            g_ref, r1.at[slot], r1_send.at[m], r1_recv.at[slot],
-            device_id=dev(2 * line + p, b, c), device_id_type=MESH,
-        ).wait_recv()
-    tot_ref[0, 0] = (r1[0] + r1[1]) + (r1[2] + r1[3])
-    tot_ref[0, 1] = (r1[4] + r1[5]) + (r1[6] + r1[7])
-    base = 0
-    for r, ((stride, radix), (digit, peers)) in enumerate(zip(rounds, hops)):
-        here = base + digit
-        later[here] = tot_ref[r]
-        for o, (there, d) in enumerate(peers):
-            copy = pltpu.make_async_remote_copy(
-                tot_ref.at[r], later.at[here], later_send.at[base + o], later_recv.at[here],
-                device_id=d, device_id_type=MESH,
-            )
-            copy.start()
-            sends.append(copy)
-        for o, (there, d) in enumerate(peers):
-            pltpu.make_async_remote_copy(
-                tot_ref.at[r], later.at[base + there], later_send.at[base + o],
-                later_recv.at[base + there], device_id=d, device_id_type=MESH,
-            ).wait_recv()
-        total = later[base]
-        for o in range(1, radix):
-            total = total + later[base + o]
-        tot_ref[r + 1] = total
-        base += radix
-    done = len(rounds)
-    square = jnp.sum(tot_ref[done] * tot_ref[done], keepdims=True).reshape(1, 1)
+    def share(there, device, slot):
+        return pltpu.make_async_remote_copy(
+            g_ref, all_g.at[slot], g_send.at[there], g_recv.at[slot],
+            device_id=device, device_id_type=MESH,
+        )
+
+    def send_member(m, _):
+        there, device = member(m)
+        share(there, device, me).start()
+        return 0
+
+    def take_member(m, _):
+        there, device = member(m)
+        share(there, device, there).wait_recv()
+        return 0
+
+    lax.fori_loop(1, members, send_member, 0)
+    all_g[me] = g_ref[...]
+    lax.fori_loop(1, members, take_member, 0)
+    tot_ref[0] = jnp.sum(all_g[...], axis=0)
+    to_twin = pltpu.make_async_remote_copy(
+        tot_ref.at[0], tot_ref.at[1], twin_sem.at[0], twin_sem.at[1], device_id=twin,
+        device_id_type=MESH,
+    )
+    to_twin.start()
+    to_twin.wait_recv()
+    square = jnp.sum(tot_ref[...] * tot_ref[...], keepdims=True).reshape(1, 1)
     limit = jnp.sqrt(jnp.float32(tiles * LANES * n_chan))
     scale = jnp.minimum(1.0, limit / jnp.sqrt(square + 1e-06))
-    rows = tot_ref[done, cha] * scale
+    rows = tot_ref[0] * scale
     rows = jnp.broadcast_to(rows[:, None, :], (tiles, per, LANES)).reshape(groups, LANES)
     rows = jnp.concatenate(split3(jnp.where(row_group, rows, 0.0)), axis=1)
     upd_ref[...] = dot(jnp.concatenate([mode_hot] * 3, axis=1), rows, NT)
 
-    for copy in sends:
-        copy.wait_send()
+    def sent_member(m, _):
+        there, device = member(m)
+        share(there, device, me).wait_send()
+        return 0
+
+    lax.fori_loop(1, members, sent_member, 0)
+    to_twin.wait_send()
     to_mate.wait_send()
     for k in range(CHUNKS):
         back_copy(k).wait_send()
@@ -390,18 +376,13 @@
     tiles = chans // LANES
     half = tiles // 2
     pairs = sizes[0] // 2
-    rounds, stride = [], 1
-    while stride < pairs:
-        radix = 4 if (pairs // stride) % 4 == 0 else 2
-        rounds.append((stride, radix))
-        stride *= radix
-    slots = max(1, sum(r for _, r in rounds))
+    members = sizes[0] * sizes[1]
     part = half * LANES // CHUNKS
     wide = half * LANES
     vmem = pl.BlockSpec(memory_space=pltpu.VMEM)
     dma = pltpu.SemaphoreType.DMA
     output, update = pl.pallas_call(
-        functools.partial(kernel, sizes, rounds, width, modes),
+        functools.partial(kernel, sizes, width, modes),
         out_shape=(
             jax.ShapeDtypeStruct((steps, chans), BF16),
             jax.ShapeDtypeStruct((modes, groups), F32),
@@ -434,19 +415,17 @@
             pltpu.VMEM((tiles, steps, LANES), F32),
             pltpu.VMEM((tiles, steps, LANES), F32),
             pltpu.VMEM((tiles, LANES), F32),
-            pltpu.VMEM((8, tiles, LANES), F32),
-            pltpu.VMEM((len(rounds) + 1, 2, tiles, LANES), F32),
-            pltpu.VMEM((slots, 2, tiles, LANES), F32),
+            pltpu.VMEM((members, tiles, LANES), F32),
+            pltpu.VMEM((2, tiles, LANES), F32),
             dma((2,)),
             dma((2, CHUNKS)),
             dma((2, CHUNKS)),
-            dma((7,)),
-            dma((8,)),
-            dma((slots,)),
-            dma((slots,)),
+            dma((members,)),
+            dma((members,)),
+            dma((2,)),
         ],
         compiler_params=pltpu.CompilerParams(
-            collective_id=0, has_side_effects=True, vmem_limit_bytes=48 * 1024 * 1024
+            collective_id=0, has_side_effects=True, vmem_limit_bytes=60 * 1024 * 1024
         ),
     )(
         gated_input.reshape(steps, chans),

time: 37.4 us -> 32.7 us (0.87)
  local copies, waits for them, and re-layouts: 6.6 us -> 2.49 us
  Pallas kernels: 29.7 us -> 29 us
    unnamed x14 -> x4, local copies, waits for them, and re-layouts: 6.6 us -> 2.49 us
    pallas_call x1, Pallas kernels: 29.7 us -> 29 us  [on_device(): pl.pallas_call(functools.partial(kernel, sizes, width, modes), out_shape=...]
where the time goes in v3:
time: 32.7 us; the launch traced here: 32.2 us
  Pallas kernels  29 us (89%)
  local copies, waits for them, and re-layouts  2.49 us (8%)
  between operations  0.65 us (2%)
    pallas_call x1, Pallas kernels, on_device(): pl.pallas_call(functools.partial(kernel, sizes, width, modes), out_shape=...  29 us
    unnamed x4, local copies, waits for them, and re-layouts  2.49 us

profile of v3, /device:TPU:0, one launch (start us, length us, event | category | flops | bytes accessed | tf_op | source)
XLA Modules:
  0.0 32.2 jit_solution(1236378919168367906)
XLA Ops:
  0.6 29.0 %shard_map.77 = (bf16[128,2048]{1,0:T(8,128)(2,1)}, f32[16,128]{1,0:T(8,128)}) custom-call(bf16[128,2048]{1,0:T(8,128)(2,1)} %bitcast.8, bf16[128,2048]{1,0:T(8,128)(2,1)} %bitcast.9, bf16[128,2048]{1,0:T(8,128)(2,1)} %bitcast.10, f32[1,2048]{1,0:T(1,128)} %bitcast.12, f32[16,128]{1,0:T(8,128)} %bitcast.13, f32[16,128]{1,0:T(8,128)} %bitcast.14), custom_call_target="tpu_custom_call" | custom-call | tf_op jit(solution)/shard_map/pallas_call | solution.py:384
  29.7 0.0 copy-start
  29.7 1.9 %copy.10 = bf16[1,128,2048]{2,1,0:T(8,128)(2,1)} copy(bf16[1,128,2048]{2,1,0:T(8,128)(2,1)} %bitcast.11) | data formatting | bytes 1048576
  31.6 0.0 copy-done
  31.6 0.6 %copy.11 = f32[128,16]{0,1:T(8,128)} copy(f32[128,16]{0,1:T(8,128)S(1)} %bitcast.15) | data formatting | bytes 16384
Async XLA Ops:
  29.7 1.9 %copy-start = (f32[16,128]{1,0:T(8,128)S(1)}, f32[16,128]{1,0:T(8,128)}, u32[]{:S(2)}) copy-start(f32[16,128]{1,0:T(8,128)} %get-tuple-element.5) | copy-start | bytes 24580

commit v4 on v3

--- a/solution.py
+++ b/solution.py
@@ -47,7 +47,7 @@
     x_hbm, q_hbm, ct_hbm, skip_hbm, res_hbm, rate_hbm,
     out_ref, upd_ref,
     x_ref, q_ref, ct_ref, skip_ref, res_in, rate_in, res_ref, rate_ref, in_sem,
-    s_ref, from_mate, dec_ref, filt_ref, q_sum, even_part, chain_in, chain_out,
+    s_ref, from_mate, dec_ref, filt_ref, q_sum, even_part, chain_in,
     own_c, mate_c, other_c, near_ref, grad_in, sd_ref, fall_ref, g_ref, all_g, tot_ref,
     mate_sem, chain_sem, back_sem, g_send, g_recv, twin_sem,
 ):
@@ -189,10 +189,10 @@
 
     part = half * LANES // CHUNKS
 
-    def chain_copy(k):
+    def line_copy(slot, there):
         return pltpu.make_async_remote_copy(
-            chain_out.at[k], chain_in.at[k], chain_sem.at[0, k], chain_sem.at[1, k],
-            device_id=dev(jnp.minimum(seq + 2, n_seq - 1 - (1 - parity))), device_id_type=MESH,
+            q_sum, chain_in.at[slot], chain_sem.at[0, there], chain_sem.at[1, slot],
+            device_id=dev(2 * there + parity), device_id_type=MESH,
         )
 
     def back_copy(k):
@@ -201,7 +201,7 @@
             device_id_type=MESH,
         )
 
-    def chain_step():
+    def send_step():
         to_mate.wait_recv()
         for k in range(CHUNKS):
             cols = slice(k * part, (k + 1) * part)
@@ -211,32 +211,31 @@
             q_sum[:, cols] = dec_ref[parity, :, cols] * early + late
             even_part[:, cols] = early
 
+        def send_line(there, _):
+            line_copy(line, there).start()
+            return 0
+
+        lax.fori_loop(line + 1, pairs, send_line, 0)
+
+    def carry_step():
+        decay = dec_ref[parity]
+        twice = decay * decay
+
+        def take_line(slot, carry):
+            line_copy(slot, slot).wait_recv()
+            return twice * carry + chain_in[slot]
+
+        carry = lax.fori_loop(0, line, take_line, jnp.zeros((modes, half * LANES), F32))
+        after = decay * carry + even_part[...]
+        mine = jnp.where(parity == 0, carry, after)
+        his = jnp.where(parity == 0, after, carry)
         for k in range(CHUNKS):
             cols = slice(k * part, (k + 1) * part)
-            decay = dec_ref[parity, :, cols]
-            early = even_part[:, cols]
-
-            def finish(carry):
-                @pl.when(line < pairs - 1)
-                def _():
-                    chain_out[k] = decay * decay * carry + q_sum[:, cols]
-                    chain_copy(k).start()
-
-                after = decay * carry + early
-                mate_c[k] = jnp.where(parity == 0, after, carry)
-                back_copy(k).start()
-                own_c[k] = jnp.where(parity == 0, carry, after)
-
-            @pl.when(line == 0)
-            def _():
-                finish(jnp.zeros((modes, part), F32))
-
-            @pl.when(line > 0)
-            def _():
-                chain_copy(k).wait_recv()
-                finish(chain_in[k])
-
-    trigger = jnp.minimum(1 + lax.div(line * half, pairs), half - 1)
+            mate_c[k] = his[:, cols]
+            back_copy(k).start()
+            own_c[k] = mine[:, cols]
+
+    send_at, carry_at = min(1, half - 1), max(1, half - 2)
     ahead = (iota((steps, LANES), 0) + 1).astype(F32)
 
     def near_tile(i):
@@ -273,9 +272,13 @@
         g_ref[pl.ds(i, 1), :] = jnp.sum(wide * fall_ref[i], axis=0, keepdims=True)
 
     def near_two(i, _):
-        @pl.when(i == trigger)
+        @pl.when(i == send_at)
         def _():
-            chain_step()
+            send_step()
+
+        @pl.when(i == carry_at)
+        def _():
+            carry_step()
 
         near_tile(2 * i)
         near_tile(2 * i + 1)
@@ -364,9 +367,11 @@
     for k in range(CHUNKS):
         back_copy(k).wait_send()
 
-        @pl.when(line < pairs - 1)
-        def _():
-            chain_copy(k).wait_send()
+    def sent_line(there, _):
+        line_copy(line, there).wait_send()
+        return 0
+
+    lax.fori_loop(line + 1, pairs, sent_line, 0)
 
 
 def on_device(sizes, gated_input, query_gate, skip_gain, residues, decay_rates, cotangent):
@@ -405,8 +410,7 @@
             pltpu.VMEM((groups, steps), F32),
             pltpu.VMEM((modes, wide), F32),
             pltpu.VMEM((modes, wide), F32),
-            pltpu.VMEM((CHUNKS, modes, part), F32),
-            pltpu.VMEM((CHUNKS, modes, part), F32),
+            pltpu.VMEM((pairs, modes, wide), F32),
             pltpu.VMEM((CHUNKS, modes, part), F32),
             pltpu.VMEM((CHUNKS, modes, part), F32),
             pltpu.VMEM((CHUNKS, modes, part), F32),
@@ -418,7 +422,7 @@
             pltpu.VMEM((members, tiles, LANES), F32),
             pltpu.VMEM((2, tiles, LANES), F32),
             dma((2,)),
-            dma((2, CHUNKS)),
+            dma((2, pairs)),
             dma((2, CHUNKS)),
             dma((members,)),
             dma((members,)),

time: 32.7 us -> 31.8 us (0.972)
  Pallas kernels: 29 us -> 28.1 us
    pallas_call x1, Pallas kernels: 29 us -> 28.1 us  [on_device(): pl.pallas_call(functools.partial(kernel, sizes, width, modes), out_shape=...]
where the time goes in v4:
time: 31.8 us; the launch traced here: 31.3 us
  Pallas kernels  28.1 us (88%)
  local copies, waits for them, and re-layouts  2.49 us (8%)
  between operations  0.65 us (2%)
    pallas_call x1, Pallas kernels, on_device(): pl.pallas_call(functools.partial(kernel, sizes, width, modes), out_shape=...  28.1 us
    unnamed x4, local copies, waits for them, and re-layouts  2.49 us

profile of v4, /device:TPU:0, one launch (start us, length us, event | category | flops | bytes accessed | tf_op | source)
XLA Modules:
  0.0 31.3 jit_solution(17633895865410679302)
XLA Ops:
  0.6 28.1 %shard_map.77 = (bf16[128,2048]{1,0:T(8,128)(2,1)}, f32[16,128]{1,0:T(8,128)}) custom-call(bf16[128,2048]{1,0:T(8,128)(2,1)} %bitcast.8, bf16[128,2048]{1,0:T(8,128)(2,1)} %bitcast.9, bf16[128,2048]{1,0:T(8,128)(2,1)} %bitcast.10, f32[1,2048]{1,0:T(1,128)} %bitcast.12, f32[16,128]{1,0:T(8,128)} %bitcast.13, f32[16,128]{1,0:T(8,128)} %bitcast.14), custom_call_target="tpu_custom_call" | custom-call | tf_op jit(solution)/shard_map/pallas_call | solution.py:389
  28.8 0.0 copy-start
  28.8 1.9 %copy.10 = bf16[1,128,2048]{2,1,0:T(8,128)(2,1)} copy(bf16[1,128,2048]{2,1,0:T(8,128)(2,1)} %bitcast.11) | data formatting | bytes 1048576
  30.7 0.0 copy-done
  30.7 0.6 %copy.11 = f32[128,16]{0,1:T(8,128)} copy(f32[128,16]{0,1:T(8,128)S(1)} %bitcast.15) | data formatting | bytes 16384
Async XLA Ops:
  28.8 1.9 %copy-start = (f32[16,128]{1,0:T(8,128)S(1)}, f32[16,128]{1,0:T(8,128)}, u32[]{:S(2)}) copy-start(f32[16,128]{1,0:T(8,128)} %get-tuple-element.5) | copy-start | bytes 24580
